TPU v7x, 32 devices: a whole 2x2x4 slice. The times are simulated.
32 devices in a mesh: gx: 2 (over core), gy: 4 (over y, x), gz: 4 (over z).
Axes of the slice: x: 2, y: 2, z: 4, core: 2. Of those that a mesh axis runs over, the one named last changes fastest.
Arguments:
- dual_matrix: float32 [2, 4, 4, 1536, 1536], P('gx', 'gy', 'gz'), may hold values from -1 to 4, as said below
- modes: float32 [2, 4, 4, 6, 1536], P('gx', 'gy', 'gz'), may hold values from -0.15625 to 0.15625
- coarse_rows: float32 [192, 192], P(('gx', 'gy', 'gz')), may hold values from -0.2 to 0.4, as said below
- loads: float32 [2, 4, 4, 8, 6, 128], P('gx', 'gy', 'gz'), may hold values from -40 to 40
- face_counts: int32 [2, 4, 4, 3], replicated, may hold values from 32 to 128
- contact: int32 [2, 4, 4, 6, 128], P('gx', 'gy', 'gz'), may hold values 0 or 1
Outputs:
- multipliers: float32 [2, 4, 4, 8, 6, 128], P('gx', 'gy', 'gz')
- residual: float32 [2, 4, 4, 8, 6, 128], P('gx', 'gy', 'gz')
Inputs may be any that keep to these rules, and one draw needn't show every extreme that they name: `dual_matrix`: every subdomain's matrix is symmetric positive definite. `coarse_rows`: the coarse operator is symmetric positive definite.
All inputs are finite; a program needn't handle non-finite values. No bound on the sum of `contact` on one device may be relied on, other than what follows from the above.
Results may differ from a plain program's by a relative error of at most 0.0003.
Values sent between devices are 32-bit elements; how exact they have to be, the bound alone decides.
A program may use at most 128 MiB of HBM per device.

v0:
```python
import jax
import jax.numpy as jnp
from jax import lax
from jax.sharding import PartitionSpec as P

ITERS = 4
highest = lax.Precision.HIGHEST


def from_behind(block, axis, distance):
    devices = range(lax.axis_size(axis))
    route = [((i - distance) % len(devices), i) for i in devices]
    return lax.ppermute(block, axis, route)


def trade(upper_faces, lower_faces):
    from_below = [
        from_behind(upper_faces[0], "gx", 1),
        from_behind(upper_faces[1], "gy", 1),
        from_behind(upper_faces[2], "gz", 1),
    ]
    from_above = [
        from_behind(lower_faces[0], "gx", -1),
        from_behind(lower_faces[1], "gy", -1),
        from_behind(lower_faces[2], "gz", -1),
    ]
    return (from_below, from_above)


def spread_faces(owned_vec):
    upper_faces = [owned_vec[..., 2 * grid_axis + 1, :] for grid_axis in range(3)]
    lower_faces = [owned_vec[..., 2 * grid_axis, :] for grid_axis in range(3)]
    from_below, from_above = trade(upper_faces, lower_faces)
    faces = []
    for grid_axis in range(3):
        faces.append(jnp.concatenate([from_below[grid_axis], lower_faces[grid_axis]], axis=-1))
        faces.append(jnp.concatenate([upper_faces[grid_axis], from_above[grid_axis]], axis=-1))
    return jnp.stack(faces, axis=-2)


def collect_faces(local_form):
    half_width = local_form.shape[-1] // 2
    upper_faces = [local_form[..., 2 * grid_axis + 1, half_width:] for grid_axis in range(3)]
    lower_faces = [local_form[..., 2 * grid_axis, :half_width] for grid_axis in range(3)]
    from_below, from_above = trade(upper_faces, lower_faces)
    pieces = []
    for grid_axis in range(3):
        pieces.append(local_form[..., 2 * grid_axis, half_width:] + from_below[grid_axis])
        pieces.append(local_form[..., 2 * grid_axis + 1, :half_width] + from_above[grid_axis])
    return jnp.stack(pieces, axis=-2)


def coarse_weights(flattened, own_modes, coarse_rows):
    on_modes = jnp.einsum("jm,km->jk", own_modes, flattened, precision=highest)
    return jnp.dot(
        coarse_rows,
        lax.all_gather(on_modes, ("gx", "gy", "gz"), axis=0, tiled=True),
        precision=highest,
    )


def on_device(dual_matrix, modes, coarse_rows, loads, face_counts, contact):
    half_width = loads.shape[-1]
    case_count = loads.shape[3]
    grid_pos = [lax.axis_index("gx"), lax.axis_index("gy"), lax.axis_index("gz")]
    grid_sizes = [lax.axis_size("gx"), lax.axis_size("gy"), lax.axis_size("gz")]

    def counts_at(where):
        return lax.dynamic_slice(
            face_counts, (where[0], where[1], where[2], 0), (1, 1, 1, 3)
        ).reshape(3)

    own_counts = counts_at(grid_pos)
    positions = jnp.arange(half_width, dtype=jnp.int32)
    own_masks = []
    local_masks = []
    for grid_axis in range(3):
        lower_pos = list(grid_pos)
        lower_pos[grid_axis] = (grid_pos[grid_axis] - 1 + grid_sizes[grid_axis]) % grid_sizes[
            grid_axis
        ]
        lower_count = counts_at(lower_pos)[grid_axis]
        lower_row = (positions < lower_count).astype(jnp.float32)
        upper_row = (positions < own_counts[grid_axis]).astype(jnp.float32)
        own_masks.extend([lower_row, upper_row])
        local_masks.extend(
            [jnp.concatenate([lower_row, lower_row]), jnp.concatenate([upper_row, upper_row])]
        )
    active_own = jnp.stack(own_masks).reshape(1, 1, 1, 1, 6, half_width)
    is_contact = contact[:, :, :, None] == 1
    matrix = dual_matrix[0, 0, 0]
    own_modes = modes[0, 0, 0]

    def local_coarse(local_form):
        flattened = local_form.reshape(case_count, -1)
        weights = coarse_weights(flattened, own_modes, coarse_rows)
        return jnp.einsum("jk,jm->km", weights, own_modes, precision=highest).reshape(
            local_form.shape
        )

    def project(vector):
        return vector - collect_faces(local_coarse(spread_faces(vector))) * active_own

    start_vector = loads * active_own

    def partial_inner(first, second):
        return jnp.sum(first * second, axis=(0, 1, 2, 4, 5))

    multipliers = jnp.zeros(loads.shape, jnp.float32)
    residual = start_vector

    def energy_sum(first, second):
        return lax.psum(partial_inner(first, second), ("gx", "gy", "gz")).reshape(-1, 1, 1)

    precond = project(residual)
    direction = precond
    energy = energy_sum(residual, precond)
    for rounds in range(ITERS):
        local_local_form = spread_faces(direction)
        local_flattened = local_local_form.reshape(case_count, -1)
        dual_image = (
            collect_faces(
                jnp.dot(local_flattened, matrix, precision=highest).reshape(local_local_form.shape)
            )
            * active_own
        )
        curvature = lax.psum(partial_inner(direction, dual_image), ("gx", "gy", "gz")).reshape(
            -1, 1, 1
        )
        step_size = energy / curvature
        updated = multipliers + step_size * direction
        multipliers = jnp.where(is_contact, jnp.maximum(updated, 0.0), updated)
        residual = residual - step_size * dual_image
        if rounds + 1 < ITERS:
            precond = project(residual)
            energy_next = energy_sum(residual, precond)
            direction = precond + energy_next / energy * direction
            energy = energy_next
    return (multipliers, residual)


def solution(mesh):
    return jax.shard_map(
        on_device,
        mesh=mesh,
        in_specs=(
            P("gx", "gy", "gz", None, None),
            P("gx", "gy", "gz", None, None),
            P(("gx", "gy", "gz"), None),
            P("gx", "gy", "gz", None, None, None),
            P(),
            P("gx", "gy", "gz", None, None),
        ),
        out_specs=(P("gx", "gy", "gz", None, None, None), P("gx", "gy", "gz", None, None, None)),
        check_vma=False,
    )
```

profile of v0, /device:TPU:0, one launch (start us, length us, event | category | flops | bytes accessed | tf_op | source)
XLA Modules:
  0.0 787.7 jit_solution(9719686072488246595)
XLA Ops:
  18.8 67.1 %all-gather = f32[32,6,8]{2,1,0:T(8,128)S(1)} all-gather(f32[1,6,8]{2,1,0:T(8,128)S(1)} %bitcast.1086), channel_id=1, replica_groups=mesh['gx'=2,'gy'=4,'gz'=4] {'gx','gy','gz'}, dimensions={0}, use_global_device_ids=true | all-gather | bytes 6336 | tf_op jit(solution)/shard_map/all_gather | solution.py:57
  91.9 3.9 collective-permute-start.11
  95.8 4.1 collective-permute-done.9
  100.8 9.6 %copy.36 = f32[1,1,1,1536,1536]{3,4,2,1,0:T(8,128)} copy(f32[1,1,1,1536,1536]{4,3,2,1,0:T(8,128)} %param.6) | data formatting | bytes 18874368 | tf_op args[0]
  114.7 3.9 collective-permute-start.17
  120.1 10.1 %convolution_bitcast_fusion.6 = f32[1,1,1,8,6,256]{5,3,4,2,1,0:T(8,128)S(1)} fusion(f32[8,1536,1]{1,0,2:T(8,128)S(1)} %bitcast.1078, f32[6,256,1536]{2,1,0:T(8,128)} %bitcast.1070), kind=kOutput, calls=%fused_computation.6 | convolution fusion | flops 226492416 | bytes 9535488 | tf_op jit(solution)/shard_map/dot_general | solution.py:123
  139.4 41.9 %all-reduce = (f32[8]{0:T(128)S(1)}, f32[8]{0:T(128)S(1)}) all-reduce(f32[8]{0:T(128)S(1)} %get-tuple-element.3, f32[8]{0:T(128)S(1)} %get-tuple-element.2), channel_id=1, replica_groups=mesh['gx'=2,'gy'=4,'gz'=4] {'gx','gy','gz'}, use_global_device_ids=true, to_apply=%region_1.2 | all-reduce | flops 16 | bytes 128 | tf_op jit(solution)/shard_map/psum | solution.py:113
  191.2 67.3 %all-gather.1 = f32[32,6,8]{2,1,0:T(8,128)S(1)} all-gather(f32[1,6,8]{2,1,0:T(8,128)S(1)} %bitcast.1087), channel_id=1, replica_groups=mesh['gx'=2,'gy'=4,'gz'=4] {'gx','gy','gz'}, dimensions={0}, use_global_device_ids=true | all-gather | bytes 6336 | tf_op jit(solution)/shard_map/all_gather | solution.py:57
  264.6 3.8 collective-permute-start.35
  272.2 42.4 %psum.58 = f32[8]{0:T(128)S(1)} all-reduce(f32[8]{0:T(128)S(1)} %multiply_reduce_fusion.5), channel_id=1, replica_groups=mesh['gx'=2,'gy'=4,'gz'=4] {'gx','gy','gz'}, use_global_device_ids=true, to_apply=%region_5.6 | all-reduce | flops 8 | bytes 64 | tf_op jit(solution)/shard_map/psum | solution.py:113
  324.7 10.1 %convolution_bitcast_fusion.4 = f32[1,1,1,8,6,256]{5,3,4,2,1,0:T(8,128)S(1)} fusion(f32[8,1536,1]{1,0,2:T(8,128)S(1)} %bitcast.1079, f32[6,256,1536]{2,1,0:T(8,128)} %bitcast.1071), kind=kOutput, calls=%fused_computation.4 | convolution fusion | flops 226492416 | bytes 9535488 | tf_op jit(solution)/shard_map/dot_general | solution.py:123
  343.8 39.2 %psum.59 = f32[8]{0:T(128)S(1)} all-reduce(f32[8]{0:T(128)S(1)} %multiply_reduce_fusion.4), channel_id=1, replica_groups=mesh['gx'=2,'gy'=4,'gz'=4] {'gx','gy','gz'}, use_global_device_ids=true, to_apply=%region_7.8 | all-reduce | flops 8 | bytes 64 | tf_op jit(solution)/shard_map/psum | solution.py:127
  393.0 66.9 %all-gather.2 = f32[32,6,8]{2,1,0:T(8,128)S(1)} all-gather(f32[1,6,8]{2,1,0:T(8,128)S(1)} %bitcast.1088), channel_id=1, replica_groups=mesh['gx'=2,'gy'=4,'gz'=4] {'gx','gy','gz'}, dimensions={0}, use_global_device_ids=true | all-gather | bytes 6336 | tf_op jit(solution)/shard_map/all_gather | solution.py:57
  466.0 3.8 collective-permute-start.59
  469.8 4.1 collective-permute-done.57
  474.1 42.4 %psum.60 = f32[8]{0:T(128)S(1)} all-reduce(f32[8]{0:T(128)S(1)} %multiply_reduce_fusion.3), channel_id=1, replica_groups=mesh['gx'=2,'gy'=4,'gz'=4] {'gx','gy','gz'}, use_global_device_ids=true, to_apply=%region_9.10 | all-reduce | flops 8 | bytes 64 | tf_op jit(solution)/shard_map/psum | solution.py:113
  526.6 10.1 %convolution_bitcast_fusion.2 = f32[1,1,1,8,6,256]{5,3,4,2,1,0:T(8,128)S(1)} fusion(f32[8,1536,1]{1,0,2:T(8,128)S(1)} %bitcast.1080, f32[6,256,1536]{2,1,0:T(8,128)} %bitcast.1072), kind=kOutput, calls=%fused_computation.2 | convolution fusion | flops 226492416 | bytes 9535488 | tf_op jit(solution)/shard_map/dot_general | solution.py:123
  545.7 39.2 %psum.61 = f32[8]{0:T(128)S(1)} all-reduce(f32[8]{0:T(128)S(1)} %multiply_reduce_fusion.2), channel_id=1, replica_groups=mesh['gx'=2,'gy'=4,'gz'=4] {'gx','gy','gz'}, use_global_device_ids=true, to_apply=%region_11.12 | all-reduce | flops 8 | bytes 64 | tf_op jit(solution)/shard_map/psum | solution.py:127
  594.9 66.9 %all-gather.3 = f32[32,6,8]{2,1,0:T(8,128)S(1)} all-gather(f32[1,6,8]{2,1,0:T(8,128)S(1)} %bitcast.1089), channel_id=1, replica_groups=mesh['gx'=2,'gy'=4,'gz'=4] {'gx','gy','gz'}, dimensions={0}, use_global_device_ids=true | all-gather | bytes 6336 | tf_op jit(solution)/shard_map/all_gather | solution.py:57
  667.9 3.8 collective-permute-start.83
  671.7 4.1 collective-permute-done.81
  676.0 42.4 %psum.62 = f32[8]{0:T(128)S(1)} all-reduce(f32[8]{0:T(128)S(1)} %multiply_reduce_fusion.1), channel_id=1, replica_groups=mesh['gx'=2,'gy'=4,'gz'=4] {'gx','gy','gz'}, use_global_device_ids=true, to_apply=%region_13.14 | all-reduce | flops 8 | bytes 64 | tf_op jit(solution)/shard_map/psum | solution.py:113
  728.5 10.1 %convolution_bitcast_fusion = f32[1,1,1,8,6,256]{5,3,4,2,1,0:T(8,128)S(1)} fusion(f32[8,1536,1]{1,0,2:T(8,128)S(1)} %bitcast.1081, f32[6,256,1536]{2,1,0:T(8,128)} %bitcast.1073), kind=kOutput, calls=%fused_computation | convolution fusion | flops 226492416 | bytes 9535488 | tf_op jit(solution)/shard_map/dot_general | solution.py:123
  747.7 39.3 %psum.63 = f32[8]{0:T(128)S(1)} all-reduce(f32[8]{0:T(128)S(1)} %multiply_reduce_fusion), channel_id=1, replica_groups=mesh['gx'=2,'gy'=4,'gz'=4] {'gx','gy','gz'}, use_global_device_ids=true, to_apply=%region_15.16 | all-reduce | flops 8 | bytes 64 | tf_op jit(solution)/shard_map/psum | solution.py:127
  (356 shorter events, 149.5 us)
Async XLA Ops:
  7.3 8.9 %collective-permute-start.1 = (f32[1,1,1,8,128]{4,3,2,1,0:T(8,128)S(1)}, f32[1,1,1,8,128]{4,3,2,1,0:T(8,128)S(1)}, u32[]{:S(2)}, u32[]{:S(2)}) collective-permute-start(f32[1,1,1,8,128]{4,3,2,1,0:T(8,128)S(1)} %get-tuple-element.100), channel_id=1, source_target_pairs={{16,0},{0,16},{17,1},{1,17},{18,2},{2,18},{19,3},{3,19},{20,4},{4,... | collective-permute-start | bytes 12296 | tf_op jit(solution)/shard_map/ppermute | solution.py:13
  7.4 8.8 %collective-permute-start.2 = (f32[1,1,1,8,128]{4,3,2,1,0:T(8,128)S(1)}, f32[1,1,1,8,128]{4,3,2,1,0:T(8,128)S(1)}, u32[]{:S(2)}, u32[]{:S(2)}) collective-permute-start(f32[1,1,1,8,128]{4,3,2,1,0:T(8,128)S(1)} %get-tuple-element.99), channel_id=1, source_target_pairs={{12,0},{0,4},{4,8},{8,12},{13,1},{1,5},{5,9},{9,13},{14,2},{2,6},{... | collective-permute-start | bytes 12296 | tf_op jit(solution)/shard_map/ppermute | solution.py:13
  90.6 9.4 %collective-permute-start.9 = (f32[1,1,1,8,128]{4,3,2,1,0:T(8,128)S(1)}, f32[1,1,1,8,128]{4,3,2,1,0:T(8,128)S(1)}, u32[]{:S(2)}, u32[]{:S(2)}) collective-permute-start(f32[1,1,1,8,128]{4,3,2,1,0:T(8,128)S(1)} %get-tuple-element.50), channel_id=1, source_target_pairs={{4,0},{8,4},{12,8},{0,12},{5,1},{9,5},{13,9},{1,13},{6,2},{10,6},{... | collective-permute-start | bytes 12296 | tf_op jit(solution)/shard_map/ppermute | solution.py:13
  91.9 8.0 %collective-permute-start.10 = (f32[1,1,1,8,128]{4,3,2,1,0:T(8,128)S(1)}, f32[1,1,1,8,128]{4,3,2,1,0:T(8,128)S(1)}, u32[]{:S(2)}, u32[]{:S(2)}) collective-permute-start(f32[1,1,1,8,128]{4,3,2,1,0:T(8,128)S(1)} %get-tuple-element.49), channel_id=1, source_target_pairs={{3,0},{0,1},{1,2},{2,3},{7,4},{4,5},{5,6},{6,7},{11,8},{8,9},{9,10... | collective-permute-start | bytes 12296 | tf_op jit(solution)/shard_map/ppermute | solution.py:13
  91.9 8.0 %collective-permute-start.11 = (f32[1,1,1,8,128]{4,3,2,1,0:T(8,128)S(1)}, f32[1,1,1,8,128]{4,3,2,1,0:T(8,128)S(1)}, u32[]{:S(2)}, u32[]{:S(2)}) collective-permute-start(f32[1,1,1,8,128]{4,3,2,1,0:T(8,128)S(1)} %get-tuple-element.48), channel_id=1, source_target_pairs={{1,0},{2,1},{3,2},{0,3},{5,4},{6,5},{7,6},{4,7},{9,8},{10,9},{11,1... | collective-permute-start | bytes 12296 | tf_op jit(solution)/shard_map/ppermute | solution.py:13
  100.7 14.0 %collective-permute-start.12 = (f32[1,1,1,8,128]{4,3,2,1,0:T(8,128)S(1)}, f32[1,1,1,8,128]{4,3,2,1,0:T(8,128)S(1)}, u32[]{:S(2)}, u32[]{:S(2)}) collective-permute-start(f32[1,1,1,8,128]{4,3,2,1,0:T(8,128)S(1)} %get-tuple-element.95), channel_id=1, source_target_pairs={{16,0},{0,16},{17,1},{1,17},{18,2},{2,18},{19,3},{3,19},{20,4},{4,... | collective-permute-start | bytes 12296 | tf_op jit(solution)/shard_map/ppermute | solution.py:13
  110.5 8.1 %collective-permute-start.13 = (f32[1,1,1,8,128]{4,3,2,1,0:T(8,128)S(1)}, f32[1,1,1,8,128]{4,3,2,1,0:T(8,128)S(1)}, u32[]{:S(2)}, u32[]{:S(2)}) collective-permute-start(f32[1,1,1,8,128]{4,3,2,1,0:T(8,128)S(1)} %get-tuple-element.94), channel_id=1, source_target_pairs={{16,0},{0,16},{17,1},{1,17},{18,2},{2,18},{19,3},{3,19},{20,4},{4,... | collective-permute-start | bytes 12296 | tf_op jit(solution)/shard_map/ppermute | solution.py:13
  110.9 7.7 collective-permute-start.14
  181.4 8.0 %collective-permute-start.25 = (f32[1,1,1,8,128]{4,3,2,1,0:T(8,128)S(1)}, f32[1,1,1,8,128]{4,3,2,1,0:T(8,128)S(1)}, u32[]{:S(2)}, u32[]{:S(2)}) collective-permute-start(f32[1,1,1,8,128]{4,3,2,1,0:T(8,128)S(1)} %get-tuple-element.88), channel_id=1, source_target_pairs={{16,0},{0,16},{17,1},{1,17},{18,2},{2,18},{19,3},{3,19},{20,4},{4,... | collective-permute-start | bytes 12296 | tf_op jit(solution)/shard_map/ppermute | solution.py:13
  262.7 9.4 %collective-permute-start.33 = (f32[1,1,1,8,128]{4,3,2,1,0:T(8,128)S(1)}, f32[1,1,1,8,128]{4,3,2,1,0:T(8,128)S(1)}, u32[]{:S(2)}, u32[]{:S(2)}) collective-permute-start(f32[1,1,1,8,128]{4,3,2,1,0:T(8,128)S(1)} %get-tuple-element.38), channel_id=1, source_target_pairs={{4,0},{8,4},{12,8},{0,12},{5,1},{9,5},{13,9},{1,13},{6,2},{10,6},{... | collective-permute-start | bytes 12296 | tf_op jit(solution)/shard_map/ppermute | solution.py:13
  314.7 8.1 %collective-permute-start.37 = (f32[1,1,1,8,128]{4,3,2,1,0:T(8,128)S(1)}, f32[1,1,1,8,128]{4,3,2,1,0:T(8,128)S(1)}, u32[]{:S(2)}, u32[]{:S(2)}) collective-permute-start(f32[1,1,1,8,128]{4,3,2,1,0:T(8,128)S(1)} %get-tuple-element.82), channel_id=1, source_target_pairs={{16,0},{0,16},{17,1},{1,17},{18,2},{2,18},{19,3},{3,19},{20,4},{4,... | collective-permute-start | bytes 12296 | tf_op jit(solution)/shard_map/ppermute | solution.py:13
  315.2 7.6 collective-permute-start.38
  383.2 7.5 collective-permute-start.49
  464.5 9.4 %collective-permute-start.57 = (f32[1,1,1,8,128]{4,3,2,1,0:T(8,128)S(1)}, f32[1,1,1,8,128]{4,3,2,1,0:T(8,128)S(1)}, u32[]{:S(2)}, u32[]{:S(2)}) collective-permute-start(f32[1,1,1,8,128]{4,3,2,1,0:T(8,128)S(1)} %get-tuple-element.26), channel_id=1, source_target_pairs={{4,0},{8,4},{12,8},{0,12},{5,1},{9,5},{13,9},{1,13},{6,2},{10,6},{... | collective-permute-start | bytes 12296 | tf_op jit(solution)/shard_map/ppermute | solution.py:13
  466.0 8.0 %collective-permute-start.58 = (f32[1,1,1,8,128]{4,3,2,1,0:T(8,128)S(1)}, f32[1,1,1,8,128]{4,3,2,1,0:T(8,128)S(1)}, u32[]{:S(2)}, u32[]{:S(2)}) collective-permute-start(f32[1,1,1,8,128]{4,3,2,1,0:T(8,128)S(1)} %get-tuple-element.25), channel_id=1, source_target_pairs={{3,0},{0,1},{1,2},{2,3},{7,4},{4,5},{5,6},{6,7},{11,8},{8,9},{9,10... | collective-permute-start | bytes 12296 | tf_op jit(solution)/shard_map/ppermute | solution.py:13
  466.0 8.0 %collective-permute-start.59 = (f32[1,1,1,8,128]{4,3,2,1,0:T(8,128)S(1)}, f32[1,1,1,8,128]{4,3,2,1,0:T(8,128)S(1)}, u32[]{:S(2)}, u32[]{:S(2)}) collective-permute-start(f32[1,1,1,8,128]{4,3,2,1,0:T(8,128)S(1)} %get-tuple-element.24), channel_id=1, source_target_pairs={{1,0},{2,1},{3,2},{0,3},{5,4},{6,5},{7,6},{4,7},{9,8},{10,9},{11,1... | collective-permute-start | bytes 12296 | tf_op jit(solution)/shard_map/ppermute | solution.py:13
  516.6 8.1 %collective-permute-start.61 = (f32[1,1,1,8,128]{4,3,2,1,0:T(8,128)S(1)}, f32[1,1,1,8,128]{4,3,2,1,0:T(8,128)S(1)}, u32[]{:S(2)}, u32[]{:S(2)}) collective-permute-start(f32[1,1,1,8,128]{4,3,2,1,0:T(8,128)S(1)} %get-tuple-element.70), channel_id=1, source_target_pairs={{16,0},{0,16},{17,1},{1,17},{18,2},{2,18},{19,3},{3,19},{20,4},{4,... | collective-permute-start | bytes 12296 | tf_op jit(solution)/shard_map/ppermute | solution.py:13
  517.1 7.6 collective-permute-start.62
  585.1 7.5 collective-permute-start.73
  666.4 9.4 %collective-permute-start.81 = (f32[1,1,1,8,128]{4,3,2,1,0:T(8,128)S(1)}, f32[1,1,1,8,128]{4,3,2,1,0:T(8,128)S(1)}, u32[]{:S(2)}, u32[]{:S(2)}) collective-permute-start(f32[1,1,1,8,128]{4,3,2,1,0:T(8,128)S(1)} %get-tuple-element.14), channel_id=1, source_target_pairs={{4,0},{8,4},{12,8},{0,12},{5,1},{9,5},{13,9},{1,13},{6,2},{10,6},{... | collective-permute-start | bytes 12296 | tf_op jit(solution)/shard_map/ppermute | solution.py:13
  667.9 8.0 %collective-permute-start.82 = (f32[1,1,1,8,128]{4,3,2,1,0:T(8,128)S(1)}, f32[1,1,1,8,128]{4,3,2,1,0:T(8,128)S(1)}, u32[]{:S(2)}, u32[]{:S(2)}) collective-permute-start(f32[1,1,1,8,128]{4,3,2,1,0:T(8,128)S(1)} %get-tuple-element.13), channel_id=1, source_target_pairs={{3,0},{0,1},{1,2},{2,3},{7,4},{4,5},{5,6},{6,7},{11,8},{8,9},{9,10... | collective-permute-start | bytes 12296 | tf_op jit(solution)/shard_map/ppermute | solution.py:13
  667.9 8.0 %collective-permute-start.83 = (f32[1,1,1,8,128]{4,3,2,1,0:T(8,128)S(1)}, f32[1,1,1,8,128]{4,3,2,1,0:T(8,128)S(1)}, u32[]{:S(2)}, u32[]{:S(2)}) collective-permute-start(f32[1,1,1,8,128]{4,3,2,1,0:T(8,128)S(1)} %get-tuple-element.12), channel_id=1, source_target_pairs={{1,0},{2,1},{3,2},{0,3},{5,4},{6,5},{7,6},{4,7},{9,8},{10,9},{11,1... | collective-permute-start | bytes 12296 | tf_op jit(solution)/shard_map/ppermute | solution.py:13
  718.5 8.1 %collective-permute-start.85 = (f32[1,1,1,8,128]{4,3,2,1,0:T(8,128)S(1)}, f32[1,1,1,8,128]{4,3,2,1,0:T(8,128)S(1)}, u32[]{:S(2)}, u32[]{:S(2)}) collective-permute-start(f32[1,1,1,8,128]{4,3,2,1,0:T(8,128)S(1)} %get-tuple-element.58), channel_id=1, source_target_pairs={{16,0},{0,16},{17,1},{1,17},{18,2},{2,18},{19,3},{3,19},{20,4},{4,... | collective-permute-start | bytes 12296 | tf_op jit(solution)/shard_map/ppermute | solution.py:13
  719.0 7.6 collective-permute-start.86
  (76 other events, 816.4 us)
where the time goes:
time: 789 us; the launch traced here: 788 us
  blocking collectives  555 us (70%)
  starting transfers between devices  131 us (17%)
  matrix products  43.7 us (6%)
  waiting for transfers between devices  36.2 us (5%)
  local copies, waits for them, and re-layouts  12.5 us (2%)
    all_gather x4, blocking collectives, coarse_weights(): lax.all_gather(on_modes, ('gx', 'gy', 'gz'), axis=0, tiled=True)  268 us
    psum x4, blocking collectives, energy_sum(): lax.psum(partial_inner(first, second), ('gx', 'gy', 'gz')).reshape(-1, 1, 1)  169 us
    ppermute x96, starting transfers between devices, from_behind(): return lax.ppermute(block, axis, route)  131 us
    psum x3, blocking collectives, on_device(): lax.psum(partial_inner(direction, dual_image), ('gx', 'gy', 'gz'))  118 us
    dot_general x4, matrix products, on_device(): jnp.dot(local_flattened, matrix, precision=highest)  40.3 us
    ppermute x96, waiting for transfers between devices, from_behind(): return lax.ppermute(block, axis, route)  36.2 us
  transfers between devices with their start and end apart: 96, of which 24 were waited for; matrix products, arithmetic and copies ran while one was open for 1% of the time, Pallas kernels for 0%

commit v1 on v0

--- a/solution.py
+++ b/solution.py
@@ -5,6 +5,32 @@
 
 ITERS = 4
 highest = lax.Precision.HIGHEST
+
+
+def ways_write(here_x, dim_at):
+    here_x = jnp.moveaxis(here_x, 0, dim_at)
+    shaped = here_x.shape
+    mat_out = here_x.reshape(
+        *shaped[:dim_at], shaped[dim_at] * shaped[dim_at + 1], *shaped[dim_at + 2 :]
+    )
+    return mat_out
+
+
+def track_loops(base_x, chip_axis):
+    dev_count = lax.axis_size(chip_axis)
+    main = base_x[None]
+    for p in range(dev_count.bit_length() - 1):
+        e_now = 1 << p
+        later = lax.ppermute(main, chip_axis, [(jj, jj ^ e_now) for jj in range(dev_count)])
+        newest = jnp.stack([main, later])
+        small = lax.axis_index(chip_axis) >> p & 1
+        main = jnp.where(small == 0, newest, newest[::-1]).reshape(-1, *base_x.shape)
+    return main
+
+
+def run_racks(page, in_dim, u):
+    upper = ways_write(track_loops(page, u), in_dim)
+    return upper
 
 
 def from_behind(block, axis, distance):
@@ -52,11 +78,7 @@
 
 def coarse_weights(flattened, own_modes, coarse_rows):
     on_modes = jnp.einsum("jm,km->jk", own_modes, flattened, precision=highest)
-    return jnp.dot(
-        coarse_rows,
-        lax.all_gather(on_modes, ("gx", "gy", "gz"), axis=0, tiled=True),
-        precision=highest,
-    )
+    return jnp.dot(coarse_rows, run_racks(on_modes, 0, ("gx", "gy", "gz")), precision=highest)
 
 
 def on_device(dual_matrix, modes, coarse_rows, loads, face_counts, contact):

time: 789 us -> 559 us (0.71)
  blocking collectives: 555 us -> 276 us
  waiting for transfers between devices: 36.2 us -> 65.5 us
  starting transfers between devices: 131 us -> 148 us
    all_gather x4 -> x0, blocking collectives: 268 us -> none  [coarse_weights(): lax.all_gather(on_modes, ('gx', 'gy', 'gz'), axis=0, tiled=True)]
    ppermute x0 -> x20, waiting for transfers between devices: none -> 40.1 us  [track_loops(): lax.ppermute(main, chip_axis, [(jj, jj ^ e_now) for jj in range(dev_count)])]
    ppermute x0 -> x20, starting transfers between devices: none -> 27.1 us  [track_loops(): lax.ppermute(main, chip_axis, [(jj, jj ^ e_now) for jj in range(dev_count)])]
    psum x4, blocking collectives: 169 us -> 158 us  [energy_sum(): lax.psum(partial_inner(first, second), ('gx', 'gy', 'gz')).reshape(-1, 1, 1)]
    ppermute x96, waiting for transfers between devices: 36.2 us -> 25.4 us  [from_behind(): return lax.ppermute(block, axis, route)]
    ppermute x96, starting transfers between devices: 131 us -> 121 us  [from_behind(): return lax.ppermute(block, axis, route)]
  transfers between devices with their start and end apart: 96 -> 116, of which waited for: 24 -> 39; matrix products, arithmetic and copies ran while one was open for 1% -> 2% of each run, Pallas kernels for 0% -> 0%
where the time goes in v1:
time: 559 us; the launch traced here: 558 us
  blocking collectives  276 us (49%)
  starting transfers between devices  148 us (26%)
  waiting for transfers between devices  65.5 us (12%)
  matrix products  43 us (8%)
  local copies, waits for them, and re-layouts  14.8 us (3%)
  other arithmetic  7.95 us (1%)
    psum x4, blocking collectives, energy_sum(): lax.psum(partial_inner(first, second), ('gx', 'gy', 'gz')).reshape(-1, 1, 1)  158 us
    ppermute x96, starting transfers between devices, from_behind(): return lax.ppermute(block, axis, route)  121 us
    psum x3, blocking collectives, on_device(): lax.psum(partial_inner(direction, dual_image), ('gx', 'gy', 'gz'))  118 us
    dot_general x4, matrix products, on_device(): jnp.dot(local_flattened, matrix, precision=highest)  40.3 us
    ppermute x20, waiting for transfers between devices, track_loops(): lax.ppermute(main, chip_axis, [(jj, jj ^ e_now) for jj in range(dev_count)])  40.1 us
    ppermute x20, starting transfers between devices, track_loops(): lax.ppermute(main, chip_axis, [(jj, jj ^ e_now) for jj in range(dev_count)])  27.1 us
    ppermute x96, waiting for transfers between devices, from_behind(): return lax.ppermute(block, axis, route)  25.4 us
  transfers between devices with their start and end apart: 116, of which 39 were waited for; matrix products, arithmetic and copies ran while one was open for 2% of the time, Pallas kernels for 0%

profile of v1, /device:TPU:0, one launch (start us, length us, event | category | flops | bytes accessed | tf_op | source)
XLA Modules:
  0.0 557.6 jit_solution(4386805252269204090)
XLA Ops:
  7.3 2.9 collective-permute-start.2
  21.6 2.7 collective-permute-start.7
  27.0 2.9 collective-permute-done.8
  45.7 9.7 %copy.123 = f32[1,1,1,1536,1536]{3,4,2,1,0:T(8,128)} copy(f32[1,1,1,1536,1536]{4,3,2,1,0:T(8,128)} %param.6) | data formatting | bytes 18874368 | tf_op args[0]
  56.1 2.7 collective-permute-start.20
  60.2 2.5 collective-permute-start.22
  64.2 10.1 %convolution_bitcast_fusion.6 = f32[1,1,1,8,6,256]{5,3,4,2,1,0:T(8,128)S(1)} fusion(f32[8,1536,1]{1,0,2:T(8,128)S(1)} %bitcast.1178, f32[6,256,1536]{2,1,0:T(8,128)} %bitcast.1162), kind=kOutput, calls=%fused_computation.6 | convolution fusion | flops 226492416 | bytes 9535488 | tf_op jit(solution)/shard_map/dot_general | solution.py:145
  75.2 2.7 collective-permute-start.26
  79.1 2.5 collective-permute-start.28
  83.4 39.5 %all-reduce = (f32[8]{0:T(128)S(1)}, f32[8]{0:T(128)S(1)}) all-reduce(f32[8]{0:T(128)S(1)} %get-tuple-element.3, f32[8]{0:T(128)S(1)} %get-tuple-element.2), channel_id=1, replica_groups=mesh['gx'=2,'gy'=4,'gz'=4] {'gx','gy','gz'}, use_global_device_ids=true, to_apply=%region_1.2 | all-reduce | flops 16 | bytes 128 | tf_op jit(solution)/shard_map/psum | solution.py:135
  142.0 2.7 collective-permute-done.37
  159.8 39.5 %psum.58 = f32[8]{0:T(128)S(1)} all-reduce(f32[8]{0:T(128)S(1)} %multiply_reduce_fusion.5), channel_id=1, replica_groups=mesh['gx'=2,'gy'=4,'gz'=4] {'gx','gy','gz'}, use_global_device_ids=true, to_apply=%region_5.6 | all-reduce | flops 8 | bytes 64 | tf_op jit(solution)/shard_map/psum | solution.py:135
  208.9 10.1 %convolution_bitcast_fusion.4 = f32[1,1,1,8,6,256]{5,3,4,2,1,0:T(8,128)S(1)} fusion(f32[8,1536,1]{1,0,2:T(8,128)S(1)} %bitcast.1179, f32[6,256,1536]{2,1,0:T(8,128)} %bitcast.1163), kind=kOutput, calls=%fused_computation.4 | convolution fusion | flops 226492416 | bytes 9535488 | tf_op jit(solution)/shard_map/dot_general | solution.py:145
  223.9 2.5 collective-permute-start.57
  228.1 39.3 %psum.59 = f32[8]{0:T(128)S(1)} all-reduce(f32[8]{0:T(128)S(1)} %multiply_reduce_fusion.4), channel_id=1, replica_groups=mesh['gx'=2,'gy'=4,'gz'=4] {'gx','gy','gz'}, use_global_device_ids=true, to_apply=%region_7.8 | all-reduce | flops 8 | bytes 64 | tf_op jit(solution)/shard_map/psum | solution.py:149
  286.6 2.7 collective-permute-done.66
  304.4 39.6 %psum.60 = f32[8]{0:T(128)S(1)} all-reduce(f32[8]{0:T(128)S(1)} %multiply_reduce_fusion.3), channel_id=1, replica_groups=mesh['gx'=2,'gy'=4,'gz'=4] {'gx','gy','gz'}, use_global_device_ids=true, to_apply=%region_9.10 | all-reduce | flops 8 | bytes 64 | tf_op jit(solution)/shard_map/psum | solution.py:135
  353.5 10.1 %convolution_bitcast_fusion.2 = f32[1,1,1,8,6,256]{5,3,4,2,1,0:T(8,128)S(1)} fusion(f32[8,1536,1]{1,0,2:T(8,128)S(1)} %bitcast.1180, f32[6,256,1536]{2,1,0:T(8,128)} %bitcast.1164), kind=kOutput, calls=%fused_computation.2 | convolution fusion | flops 226492416 | bytes 9535488 | tf_op jit(solution)/shard_map/dot_general | solution.py:145
  372.7 39.6 %psum.61 = f32[8]{0:T(128)S(1)} all-reduce(f32[8]{0:T(128)S(1)} %multiply_reduce_fusion.2), channel_id=1, replica_groups=mesh['gx'=2,'gy'=4,'gz'=4] {'gx','gy','gz'}, use_global_device_ids=true, to_apply=%region_11.12 | all-reduce | flops 8 | bytes 64 | tf_op jit(solution)/shard_map/psum | solution.py:149
  431.4 2.7 collective-permute-done.95
  449.2 39.5 %psum.62 = f32[8]{0:T(128)S(1)} all-reduce(f32[8]{0:T(128)S(1)} %multiply_reduce_fusion.1), channel_id=1, replica_groups=mesh['gx'=2,'gy'=4,'gz'=4] {'gx','gy','gz'}, use_global_device_ids=true, to_apply=%region_13.14 | all-reduce | flops 8 | bytes 64 | tf_op jit(solution)/shard_map/psum | solution.py:135
  498.3 10.1 %convolution_bitcast_fusion = f32[1,1,1,8,6,256]{5,3,4,2,1,0:T(8,128)S(1)} fusion(f32[8,1536,1]{1,0,2:T(8,128)S(1)} %bitcast.1181, f32[6,256,1536]{2,1,0:T(8,128)} %bitcast.1165), kind=kOutput, calls=%fused_computation | convolution fusion | flops 226492416 | bytes 9535488 | tf_op jit(solution)/shard_map/dot_general | solution.py:145
  513.4 2.5 collective-permute-start.115
  517.6 39.3 %psum.63 = f32[8]{0:T(128)S(1)} all-reduce(f32[8]{0:T(128)S(1)} %multiply_reduce_fusion), channel_id=1, replica_groups=mesh['gx'=2,'gy'=4,'gz'=4] {'gx','gy','gz'}, use_global_device_ids=true, to_apply=%region_15.16 | all-reduce | flops 8 | bytes 64 | tf_op jit(solution)/shard_map/psum | solution.py:149
  (460 shorter events, 197.3 us)
Async XLA Ops:
  7.2 8.0 %collective-permute-start.1 = (f32[1,1,1,8,128]{4,3,2,1,0:T(8,128)S(1)}, f32[1,1,1,8,128]{4,3,2,1,0:T(8,128)S(1)}, u32[]{:S(2)}, u32[]{:S(2)}) collective-permute-start(f32[1,1,1,8,128]{4,3,2,1,0:T(8,128)S(1)} %get-tuple-element.100), channel_id=1, source_target_pairs={{16,0},{0,16},{17,1},{1,17},{18,2},{2,18},{19,3},{3,19},{20,4},{4,... | collective-permute-start | bytes 12296 | tf_op jit(solution)/shard_map/ppermute | solution.py:39
  7.3 8.0 %collective-permute-start.2 = (f32[1,1,1,8,128]{4,3,2,1,0:T(8,128)S(1)}, f32[1,1,1,8,128]{4,3,2,1,0:T(8,128)S(1)}, u32[]{:S(2)}, u32[]{:S(2)}) collective-permute-start(f32[1,1,1,8,128]{4,3,2,1,0:T(8,128)S(1)} %get-tuple-element.99), channel_id=1, source_target_pairs={{12,0},{0,4},{4,8},{8,12},{13,1},{1,5},{5,9},{9,13},{14,2},{2,6},{... | collective-permute-start | bytes 12296 | tf_op jit(solution)/shard_map/ppermute | solution.py:39
  36.2 7.1 %collective-permute-start.12 = (f32[1,1,1,8,128]{4,3,2,1,0:T(8,128)S(1)}, f32[1,1,1,8,128]{4,3,2,1,0:T(8,128)S(1)}, u32[]{:S(2)}, u32[]{:S(2)}) collective-permute-start(f32[1,1,1,8,128]{4,3,2,1,0:T(8,128)S(1)} %get-tuple-element.52), channel_id=1, source_target_pairs={{16,0},{0,16},{17,1},{1,17},{18,2},{2,18},{19,3},{3,19},{20,4},{4,... | collective-permute-start | bytes 12296 | tf_op jit(solution)/shard_map/ppermute | solution.py:39
  45.6 14.5 %collective-permute-start.17 = (f32[1,1,1,8,128]{4,3,2,1,0:T(8,128)S(1)}, f32[1,1,1,8,128]{4,3,2,1,0:T(8,128)S(1)}, u32[]{:S(2)}, u32[]{:S(2)}) collective-permute-start(f32[1,1,1,8,128]{4,3,2,1,0:T(8,128)S(1)} %get-tuple-element.95), channel_id=1, source_target_pairs={{16,0},{0,16},{17,1},{1,17},{18,2},{2,18},{19,3},{3,19},{20,4},{4,... | collective-permute-start | bytes 12296 | tf_op jit(solution)/shard_map/ppermute | solution.py:39
  55.4 7.3 %collective-permute-start.18 = (f32[1,1,1,8,128]{4,3,2,1,0:T(8,128)S(1)}, f32[1,1,1,8,128]{4,3,2,1,0:T(8,128)S(1)}, u32[]{:S(2)}, u32[]{:S(2)}) collective-permute-start(f32[1,1,1,8,128]{4,3,2,1,0:T(8,128)S(1)} %get-tuple-element.94), channel_id=1, source_target_pairs={{16,0},{0,16},{17,1},{1,17},{18,2},{2,18},{19,3},{3,19},{20,4},{4,... | collective-permute-start | bytes 12296 | tf_op jit(solution)/shard_map/ppermute | solution.py:39
  74.4 7.3 %collective-permute-start.24 = (f32[1,1,1,8,128]{4,3,2,1,0:T(8,128)S(1)}, f32[1,1,1,8,128]{4,3,2,1,0:T(8,128)S(1)}, u32[]{:S(2)}, u32[]{:S(2)}) collective-permute-start(f32[1,1,1,8,128]{4,3,2,1,0:T(8,128)S(1)} %get-tuple-element.46), channel_id=1, source_target_pairs={{16,0},{0,16},{17,1},{1,17},{18,2},{2,18},{19,3},{3,19},{20,4},{4,... | collective-permute-start | bytes 12296 | tf_op jit(solution)/shard_map/ppermute | solution.py:39
  123.0 7.8 %collective-permute-start.30 = (f32[1,1,1,8,128]{4,3,2,1,0:T(8,128)S(1)}, f32[1,1,1,8,128]{4,3,2,1,0:T(8,128)S(1)}, u32[]{:S(2)}, u32[]{:S(2)}) collective-permute-start(f32[1,1,1,8,128]{4,3,2,1,0:T(8,128)S(1)} %get-tuple-element.88), channel_id=1, source_target_pairs={{16,0},{0,16},{17,1},{1,17},{18,2},{2,18},{19,3},{3,19},{20,4},{4,... | collective-permute-start | bytes 12296 | tf_op jit(solution)/shard_map/ppermute | solution.py:39
  123.5 7.3 %collective-permute-start.31 = (f32[1,1,1,8,128]{4,3,2,1,0:T(8,128)S(1)}, f32[1,1,1,8,128]{4,3,2,1,0:T(8,128)S(1)}, u32[]{:S(2)}, u32[]{:S(2)}) collective-permute-start(f32[1,1,1,8,128]{4,3,2,1,0:T(8,128)S(1)} %get-tuple-element.87), channel_id=1, source_target_pairs={{12,0},{0,4},{4,8},{8,12},{13,1},{1,5},{5,9},{9,13},{14,2},{2,6},{... | collective-permute-start | bytes 12296 | tf_op jit(solution)/shard_map/ppermute | solution.py:39
  151.0 7.1 %collective-permute-start.41 = (f32[1,1,1,8,128]{4,3,2,1,0:T(8,128)S(1)}, f32[1,1,1,8,128]{4,3,2,1,0:T(8,128)S(1)}, u32[]{:S(2)}, u32[]{:S(2)}) collective-permute-start(f32[1,1,1,8,128]{4,3,2,1,0:T(8,128)S(1)} %get-tuple-element.40), channel_id=1, source_target_pairs={{16,0},{0,16},{17,1},{1,17},{18,2},{2,18},{19,3},{3,19},{20,4},{4,... | collective-permute-start | bytes 12296 | tf_op jit(solution)/shard_map/ppermute | solution.py:39
  199.5 7.7 %collective-permute-start.47 = (f32[1,1,1,8,128]{4,3,2,1,0:T(8,128)S(1)}, f32[1,1,1,8,128]{4,3,2,1,0:T(8,128)S(1)}, u32[]{:S(2)}, u32[]{:S(2)}) collective-permute-start(f32[1,1,1,8,128]{4,3,2,1,0:T(8,128)S(1)} %get-tuple-element.82), channel_id=1, source_target_pairs={{16,0},{0,16},{17,1},{1,17},{18,2},{2,18},{19,3},{3,19},{20,4},{4,... | collective-permute-start | bytes 12296 | tf_op jit(solution)/shard_map/ppermute | solution.py:39
  199.9 7.2 %collective-permute-start.48 = (f32[1,1,1,8,128]{4,3,2,1,0:T(8,128)S(1)}, f32[1,1,1,8,128]{4,3,2,1,0:T(8,128)S(1)}, u32[]{:S(2)}, u32[]{:S(2)}) collective-permute-start(f32[1,1,1,8,128]{4,3,2,1,0:T(8,128)S(1)} %get-tuple-element.81), channel_id=1, source_target_pairs={{12,0},{0,4},{4,8},{8,12},{13,1},{1,5},{5,9},{9,13},{14,2},{2,6},{... | collective-permute-start | bytes 12296 | tf_op jit(solution)/shard_map/ppermute | solution.py:39
  219.1 7.3 %collective-permute-start.53 = (f32[1,1,1,8,128]{4,3,2,1,0:T(8,128)S(1)}, f32[1,1,1,8,128]{4,3,2,1,0:T(8,128)S(1)}, u32[]{:S(2)}, u32[]{:S(2)}) collective-permute-start(f32[1,1,1,8,128]{4,3,2,1,0:T(8,128)S(1)} %get-tuple-element.34), channel_id=1, source_target_pairs={{16,0},{0,16},{17,1},{1,17},{18,2},{2,18},{19,3},{3,19},{20,4},{4,... | collective-permute-start | bytes 12296 | tf_op jit(solution)/shard_map/ppermute | solution.py:39
  267.5 7.8 %collective-permute-start.59 = (f32[1,1,1,8,128]{4,3,2,1,0:T(8,128)S(1)}, f32[1,1,1,8,128]{4,3,2,1,0:T(8,128)S(1)}, u32[]{:S(2)}, u32[]{:S(2)}) collective-permute-start(f32[1,1,1,8,128]{4,3,2,1,0:T(8,128)S(1)} %get-tuple-element.76), channel_id=1, source_target_pairs={{16,0},{0,16},{17,1},{1,17},{18,2},{2,18},{19,3},{3,19},{20,4},{4,... | collective-permute-start | bytes 12296 | tf_op jit(solution)/shard_map/ppermute | solution.py:39
  268.0 7.4 %collective-permute-start.60 = (f32[1,1,1,8,128]{4,3,2,1,0:T(8,128)S(1)}, f32[1,1,1,8,128]{4,3,2,1,0:T(8,128)S(1)}, u32[]{:S(2)}, u32[]{:S(2)}) collective-permute-start(f32[1,1,1,8,128]{4,3,2,1,0:T(8,128)S(1)} %get-tuple-element.75), channel_id=1, source_target_pairs={{12,0},{0,4},{4,8},{8,12},{13,1},{1,5},{5,9},{9,13},{14,2},{2,6},{... | collective-permute-start | bytes 12296 | tf_op jit(solution)/shard_map/ppermute | solution.py:39
  295.6 7.1 %collective-permute-start.70 = (f32[1,1,1,8,128]{4,3,2,1,0:T(8,128)S(1)}, f32[1,1,1,8,128]{4,3,2,1,0:T(8,128)S(1)}, u32[]{:S(2)}, u32[]{:S(2)}) collective-permute-start(f32[1,1,1,8,128]{4,3,2,1,0:T(8,128)S(1)} %get-tuple-element.28), channel_id=1, source_target_pairs={{16,0},{0,16},{17,1},{1,17},{18,2},{2,18},{19,3},{3,19},{20,4},{4,... | collective-permute-start | bytes 12296 | tf_op jit(solution)/shard_map/ppermute | solution.py:39
  344.0 7.7 %collective-permute-start.76 = (f32[1,1,1,8,128]{4,3,2,1,0:T(8,128)S(1)}, f32[1,1,1,8,128]{4,3,2,1,0:T(8,128)S(1)}, u32[]{:S(2)}, u32[]{:S(2)}) collective-permute-start(f32[1,1,1,8,128]{4,3,2,1,0:T(8,128)S(1)} %get-tuple-element.70), channel_id=1, source_target_pairs={{16,0},{0,16},{17,1},{1,17},{18,2},{2,18},{19,3},{3,19},{20,4},{4,... | collective-permute-start | bytes 12296 | tf_op jit(solution)/shard_map/ppermute | solution.py:39
  344.5 7.2 %collective-permute-start.77 = (f32[1,1,1,8,128]{4,3,2,1,0:T(8,128)S(1)}, f32[1,1,1,8,128]{4,3,2,1,0:T(8,128)S(1)}, u32[]{:S(2)}, u32[]{:S(2)}) collective-permute-start(f32[1,1,1,8,128]{4,3,2,1,0:T(8,128)S(1)} %get-tuple-element.69), channel_id=1, source_target_pairs={{12,0},{0,4},{4,8},{8,12},{13,1},{1,5},{5,9},{9,13},{14,2},{2,6},{... | collective-permute-start | bytes 12296 | tf_op jit(solution)/shard_map/ppermute | solution.py:39
  363.7 7.3 %collective-permute-start.82 = (f32[1,1,1,8,128]{4,3,2,1,0:T(8,128)S(1)}, f32[1,1,1,8,128]{4,3,2,1,0:T(8,128)S(1)}, u32[]{:S(2)}, u32[]{:S(2)}) collective-permute-start(f32[1,1,1,8,128]{4,3,2,1,0:T(8,128)S(1)} %get-tuple-element.22), channel_id=1, source_target_pairs={{16,0},{0,16},{17,1},{1,17},{18,2},{2,18},{19,3},{3,19},{20,4},{4,... | collective-permute-start | bytes 12296 | tf_op jit(solution)/shard_map/ppermute | solution.py:39
  412.4 7.9 %collective-permute-start.88 = (f32[1,1,1,8,128]{4,3,2,1,0:T(8,128)S(1)}, f32[1,1,1,8,128]{4,3,2,1,0:T(8,128)S(1)}, u32[]{:S(2)}, u32[]{:S(2)}) collective-permute-start(f32[1,1,1,8,128]{4,3,2,1,0:T(8,128)S(1)} %get-tuple-element.64), channel_id=1, source_target_pairs={{16,0},{0,16},{17,1},{1,17},{18,2},{2,18},{19,3},{3,19},{20,4},{4,... | collective-permute-start | bytes 12296 | tf_op jit(solution)/shard_map/ppermute | solution.py:39
  412.9 7.4 %collective-permute-start.89 = (f32[1,1,1,8,128]{4,3,2,1,0:T(8,128)S(1)}, f32[1,1,1,8,128]{4,3,2,1,0:T(8,128)S(1)}, u32[]{:S(2)}, u32[]{:S(2)}) collective-permute-start(f32[1,1,1,8,128]{4,3,2,1,0:T(8,128)S(1)} %get-tuple-element.63), channel_id=1, source_target_pairs={{12,0},{0,4},{4,8},{8,12},{13,1},{1,5},{5,9},{9,13},{14,2},{2,6},{... | collective-permute-start | bytes 12296 | tf_op jit(solution)/shard_map/ppermute | solution.py:39
  440.4 7.1 %collective-permute-start.99 = (f32[1,1,1,8,128]{4,3,2,1,0:T(8,128)S(1)}, f32[1,1,1,8,128]{4,3,2,1,0:T(8,128)S(1)}, u32[]{:S(2)}, u32[]{:S(2)}) collective-permute-start(f32[1,1,1,8,128]{4,3,2,1,0:T(8,128)S(1)} %get-tuple-element.16), channel_id=1, source_target_pairs={{16,0},{0,16},{17,1},{1,17},{18,2},{2,18},{19,3},{3,19},{20,4},{4,... | collective-permute-start | bytes 12296 | tf_op jit(solution)/shard_map/ppermute | solution.py:39
  488.9 7.6 %collective-permute-start.105 = (f32[1,1,1,8,128]{4,3,2,1,0:T(8,128)S(1)}, f32[1,1,1,8,128]{4,3,2,1,0:T(8,128)S(1)}, u32[]{:S(2)}, u32[]{:S(2)}) collective-permute-start(f32[1,1,1,8,128]{4,3,2,1,0:T(8,128)S(1)} %get-tuple-element.58), channel_id=1, source_target_pairs={{16,0},{0,16},{17,1},{1,17},{18,2},{2,18},{19,3},{3,19},{20,4},{4,... | collective-permute-start | bytes 12296 | tf_op jit(solution)/shard_map/ppermute | solution.py:39
  489.4 7.2 %collective-permute-start.106 = (f32[1,1,1,8,128]{4,3,2,1,0:T(8,128)S(1)}, f32[1,1,1,8,128]{4,3,2,1,0:T(8,128)S(1)}, u32[]{:S(2)}, u32[]{:S(2)}) collective-permute-start(f32[1,1,1,8,128]{4,3,2,1,0:T(8,128)S(1)} %get-tuple-element.57), channel_id=1, source_target_pairs={{12,0},{0,4},{4,8},{8,12},{13,1},{1,5},{5,9},{9,13},{14,2},{2,6},{... | collective-permute-start | bytes 12296 | tf_op jit(solution)/shard_map/ppermute | solution.py:39
  508.6 7.3 %collective-permute-start.111 = (f32[1,1,1,8,128]{4,3,2,1,0:T(8,128)S(1)}, f32[1,1,1,8,128]{4,3,2,1,0:T(8,128)S(1)}, u32[]{:S(2)}, u32[]{:S(2)}) collective-permute-start(f32[1,1,1,8,128]{4,3,2,1,0:T(8,128)S(1)} %get-tuple-element.10), channel_id=1, source_target_pairs={{16,0},{0,16},{17,1},{1,17},{18,2},{2,18},{19,3},{3,19},{20,4},{4,... | collective-permute-start | bytes 12296 | tf_op jit(solution)/shard_map/ppermute | solution.py:39
  (96 other events, 743.3 us)
